TPU v7x, 256 devices: a whole 4x4x8 slice. The times are simulated.
256 devices in a mesh: replica: 16 (over z, core), fsdp: 4 (over y), tensor: 4 (over x).
Axes of the slice: x: 4, y: 4, z: 8, core: 2. Of those that a mesh axis runs over, the one named last changes fastest.
Arguments:
- activations: bfloat16 [32768, 8192], P(('replica', 'fsdp', 'tensor')), may hold values from -6 to 6
- cotangent: bfloat16 [32768, 2048], P(('replica', 'fsdp'), 'tensor'), may hold values from -0.625 to 0.625
- momentum: float32 [16, 8192, 2048], P('replica', 'fsdp', 'tensor'), may hold values from -6 to 6
- band_index: int32 [16, 128, 32, 16], P('replica', 'fsdp', 'tensor'), may hold values from 0 to 975, as said below
Outputs:
- new_momentum: float32 [16, 8192, 2048], P('replica', 'fsdp', 'tensor')
- update: bfloat16 [8192, 2048], P('fsdp', 'tensor')
Inputs may be any that keep to these rules, and one draw needn't show every extreme that they name: `band_index`: within each block the 16 indices of a replica are distinct, and each is k1 * 64 + k2 with k1 and k2 below 16.
All inputs are finite; a program needn't handle non-finite values.
Results may differ from a plain program's by a relative error of at most 0.0011.
Values may be sent and summed in bfloat16 or wider, within the bound.
No kernel may reach another device: no remote copies, remote signals or barrier semaphores. Data moves between devices by JAX's collectives and lax.ppermute only.
A program may use at most 128 MiB of HBM per device.

v0:
```python
import math

import jax
import jax.numpy as jnp
from jax import lax
from jax.sharding import PartitionSpec as P

SPAN = 64
LOW = 16


decay_rate = 0.999


def cosine_table(count):
    frequency = jnp.arange(count, dtype=jnp.float32)[:, None]
    position = jnp.arange(SPAN, dtype=jnp.float32)[None, :]
    raw_table = jnp.cos(math.pi * (2.0 * position + 1.0) * frequency / (2.0 * SPAN))
    weight = jnp.where(frequency == 0, math.sqrt(1.0 / SPAN), math.sqrt(2.0 / SPAN))
    return raw_table * weight


def decode(gathered_values, gathered_index, cosine_rows):
    span_rows = gathered_values.shape[1]
    columns = gathered_values.shape[2]
    slots = jnp.arange(LOW * LOW, dtype=jnp.int32)

    def add_replica(total, item):
        replica_values, replica_index = item
        index_int = replica_index.astype(jnp.int32)
        positions = index_int // SPAN * LOW + index_int % SPAN
        onehot = (positions[..., None] == slots).astype(jnp.float32)
        placed = jnp.einsum(
            "abjc,abj->abc", onehot, replica_values, precision=lax.Precision.HIGHEST
        )
        return (total + placed, None)

    combined = jnp.zeros((span_rows, columns, LOW * LOW), jnp.float32)
    combined, unused = lax.scan(add_replica, combined, (gathered_values, gathered_index))
    return jnp.einsum(
        "ki,abkl,lj->aibj",
        cosine_rows,
        combined.reshape(span_rows, columns, LOW, LOW),
        cosine_rows,
        precision=lax.Precision.HIGHEST,
    )


def local(activations, cotangent, momentum, band_index):
    momentum_in = momentum[0]
    rows_dev, cols_dev = momentum_in.shape
    contract_rows = (((0,), (0,)), ((), ()))
    gathered = lax.all_gather(activations, "tensor", axis=0, tiled=True)
    gradient = lax.psum_scatter(
        lax.dot_general(gathered, cotangent, contract_rows, preferred_element_type=jnp.float32),
        "fsdp",
        scatter_dimension=0,
        tiled=True,
    )
    blended = decay_rate * momentum_in + gradient
    span_rows = rows_dev // SPAN
    span_cols = cols_dev // SPAN
    cosine_rows = cosine_table(LOW)
    blocks = blended.reshape(span_rows, SPAN, span_cols, SPAN)
    corner = jnp.einsum(
        "ki,aibj,lj->abkl", cosine_rows, blocks, cosine_rows, precision=lax.Precision.HIGHEST
    )
    corner = corner.reshape(span_rows, span_cols, LOW * LOW)
    own_index = band_index[0]
    positions = own_index // SPAN * LOW + own_index % SPAN
    onehot = (positions[..., None] == jnp.arange(LOW * LOW, dtype=jnp.int32)).astype(jnp.float32)
    values = jnp.einsum("abjc,abc->abj", onehot, corner, precision=lax.Precision.HIGHEST)
    kept_coeffs = jnp.einsum("abjc,abj->abc", onehot, values, precision=lax.Precision.HIGHEST)
    removed = jnp.einsum(
        "ki,abkl,lj->aibj",
        cosine_rows,
        kept_coeffs.reshape(span_rows, span_cols, LOW, LOW),
        cosine_rows,
        precision=lax.Precision.HIGHEST,
    )
    new_momentum = (blended - removed.reshape(rows_dev, cols_dev))[None]
    sent_index = own_index.astype(jnp.float32)
    pieces_out = []
    for column in range(span_cols):
        got_values, got_index = (
            lax.all_gather(values[None, :, column], "replica", axis=0, tiled=True),
            lax.all_gather(sent_index[None, :, column], "replica", axis=0, tiled=True),
        )
        pieces_out.append(decode(got_values[:, :, None, :], got_index[:, :, None, :], cosine_rows))
    spatial = jnp.concatenate(pieces_out, axis=2)
    update = spatial.reshape(rows_dev, cols_dev).astype(jnp.bfloat16)
    return (new_momentum, update)


def solution(mesh):
    in_specs = (
        P(("replica", "fsdp", "tensor"), None),
        P(("replica", "fsdp"), "tensor"),
        P("replica", "fsdp", "tensor"),
        P("replica", "fsdp", "tensor", None),
    )
    out_specs = (P("replica", "fsdp", "tensor"), P("fsdp", "tensor"))
    return jax.shard_map(local, mesh=mesh, in_specs=in_specs, out_specs=out_specs, check_vma=False)
```

profile of v0, /device:TPU:1, one launch (start us, length us, event | category | flops | bytes accessed | tf_op | source)
XLA Modules:
  0.0 621.5 jit_solution(14759762903214486139)
XLA Ops:
  8.0 91.4 %all-gather.18.cloned.1.call-done = bf16[512,8192]{1,0:T(8,128)(2,1)} async-done(((bf16[128,8192]{1,0:T(8,128)(2,1)}), bf16[512,8192]{1,0:T(8,128)(2,1)}) %all-gather.18.cloned.1.call-update) | async-done | bytes 8388624 | tf_op jit(solution)/shard_map/all_gather | solution.py:53
  99.3 11.7 %fusion.239 = f32[8192,512]{1,0:T(8,128)} fusion(bf16[512,8192]{1,0:T(8,128)(2,1)} %all-gather.18.cloned.1.call-done, bf16[512,512]{1,0:T(8,128)(2,1)S(1)} %copy-done), kind=kOutput, calls=%fused_computation.342 | convolution fusion | flops 4294967296 | bytes 25690112 | tf_op jit(solution)/shard_map/dot_general | solution.py:55
  112.0 18.7 %all-gather = f32[512,1,16]{2,1,0:T(1,128)S(1)} all-gather(f32[32,1,16]{2,1,0:T(1,128)S(1)} %get-tuple-element.833), channel_id=2, replica_groups=mesh['replica'=16,'fsdp'=4,'tensor'=4] {'replica'}, dimensions={0}, use_global_device_ids=true | all-gather | bytes 34816 | tf_op jit(solution)/shard_map/all_gather | solution.py:87
  131.5 15.7 %all-gather.2 = f32[512,1,16]{2,1,0:T(1,128)S(1)} all-gather(f32[32,1,16]{2,1,0:T(1,128)S(1)} %get-tuple-element.832), channel_id=4, replica_groups=mesh['replica'=16,'fsdp'=4,'tensor'=4] {'replica'}, dimensions={0}, use_global_device_ids=true | all-gather | bytes 34816 | tf_op jit(solution)/shard_map/all_gather | solution.py:87
  147.3 16.0 %all-gather.4 = f32[512,1,16]{2,1,0:T(1,128)S(1)} all-gather(f32[32,1,16]{2,1,0:T(1,128)S(1)} %get-tuple-element.831), channel_id=6, replica_groups=mesh['replica'=16,'fsdp'=4,'tensor'=4] {'replica'}, dimensions={0}, use_global_device_ids=true | all-gather | bytes 34816 | tf_op jit(solution)/shard_map/all_gather | solution.py:87
  163.4 15.7 %all-gather.6 = f32[512,1,16]{2,1,0:T(1,128)S(1)} all-gather(f32[32,1,16]{2,1,0:T(1,128)S(1)} %get-tuple-element.830), channel_id=8, replica_groups=mesh['replica'=16,'fsdp'=4,'tensor'=4] {'replica'}, dimensions={0}, use_global_device_ids=true | all-gather | bytes 34816 | tf_op jit(solution)/shard_map/all_gather | solution.py:87
  179.2 16.0 %all-gather.8 = f32[512,1,16]{2,1,0:T(1,128)S(1)} all-gather(f32[32,1,16]{2,1,0:T(1,128)S(1)} %get-tuple-element.829), channel_id=10, replica_groups=mesh['replica'=16,'fsdp'=4,'tensor'=4] {'replica'}, dimensions={0}, use_global_device_ids=true | all-gather | bytes 34816 | tf_op jit(solution)/shard_map/all_gather | solution.py:87
  195.3 15.7 %all-gather.10 = f32[512,1,16]{2,1,0:T(1,128)S(1)} all-gather(f32[32,1,16]{2,1,0:T(1,128)S(1)} %get-tuple-element.828), channel_id=12, replica_groups=mesh['replica'=16,'fsdp'=4,'tensor'=4] {'replica'}, dimensions={0}, use_global_device_ids=true | all-gather | bytes 34816 | tf_op jit(solution)/shard_map/all_gather | solution.py:87
  211.1 16.0 %all-gather.12 = f32[512,1,16]{2,1,0:T(1,128)S(1)} all-gather(f32[32,1,16]{2,1,0:T(1,128)S(1)} %get-tuple-element.827), channel_id=14, replica_groups=mesh['replica'=16,'fsdp'=4,'tensor'=4] {'replica'}, dimensions={0}, use_global_device_ids=true | all-gather | bytes 34816 | tf_op jit(solution)/shard_map/all_gather | solution.py:87
  227.2 15.7 %all-gather.14 = f32[512,1,16]{2,1,0:T(1,128)S(1)} all-gather(f32[32,1,16]{2,1,0:T(1,128)S(1)} %get-tuple-element.826), channel_id=16, replica_groups=mesh['replica'=16,'fsdp'=4,'tensor'=4] {'replica'}, dimensions={0}, use_global_device_ids=true | all-gather | bytes 34816 | tf_op jit(solution)/shard_map/all_gather | solution.py:87
  243.2 19.5 %reduce-scatter.2.cloned.1.call-done = f32[2048,512]{1,0:T(8,128)} async-done(((f32[8192,512]{1,0:T(8,128)}), f32[2048,512]{1,0:T(8,128)}) %reduce-scatter.2.cloned.1.call-update) | async-done | bytes 4194320 | tf_op jit(solution)/shard_map/reduce_scatter | solution.py:54
  276.5 8.4 %fusion.96 = f32[32,8,64,16]{2,3,1,0:T(8,128)S(1)} fusion(f32[32,64,8,64]{3,2,1,0:T(8,128)} %reshape.806, f32[16]{0:T(128)S(1)} %compare_select_fusion, f32[64]{0:T(128)S(1)} %add_multiply_fusion), kind=kOutput, calls=%fused_computation.176 | convolution fusion | flops 201329664 | bytes 5243200 | tf_op jit(solution)/shard_map/ki,aibj,lj->abkl/dot_general | solution.py:65
  284.9 8.4 %fusion.100 = f32[32,8,16,16]{0,3,2,1:T(8,128)S(1)} fusion(f32[32,8,64,16]{2,3,1,0:T(8,128)S(1)} %fusion.96, f32[16]{0:T(128)S(1)} %compare_select_fusion, f32[64]{0:T(128)S(1)} %add_multiply_fusion), kind=kOutput, calls=%fused_computation.184 | convolution fusion | flops 50334720 | bytes 1311040 | tf_op jit(solution)/shard_map/ki,aibj,lj->abkl/dot_general | solution.py:65
  304.7 13.4 %convolution_bitcast_fusion = f32[32,64,8,64]{3,1,2,0:T(8,128)S(1)} fusion(f32[32,8,16,64]{3,2,1,0:T(8,128)S(1)} %fusion.129, f32[16]{0:T(128)S(1)} %compare_select_fusion, f32[64]{0:T(128)S(1)} %add_multiply_fusion), kind=kOutput, calls=%fused_computation.183 | convolution fusion | flops 201329664 | bytes 5243200 | tf_op jit(solution)/shard_map/ki,abkl,lj->aibj/dot_general | solution.py:74
  318.1 11.3 %copy.63 = f32[32,64,8,64]{3,2,1,0:T(8,128)} copy(f32[32,64,8,64]{3,1,2,0:T(8,128)S(1)} %convolution_bitcast_fusion) | data formatting | bytes 8388608 | tf_op jit(solution)/shard_map/ki,abkl,lj->aibj/transpose | solution.py:74
  343.4 18.6 %all-gather.1 = f32[512,1,16]{2,1,0:T(1,128)S(1)} all-gather(f32[32,1,16]{2,1,0:T(1,128)S(1)} %get-tuple-element.825), channel_id=3, replica_groups=mesh['replica'=16,'fsdp'=4,'tensor'=4] {'replica'}, dimensions={0}, use_global_device_ids=true | all-gather | bytes 34816 | tf_op jit(solution)/shard_map/all_gather | solution.py:86
  362.1 21.5 %while.104 = (s32[]{:T(128)}, f32[32,1,256]{2,1,0:T(1,128)S(1)}, f32[16,32,1,16]{1,3,2,0:T(8,128)}, f32[16,32,1,16]{1,3,2,0:T(8,128)S(1)}, s32[]{:T(128)}, /*index=5*/s32[]{:T(128)}) while((s32[]{:T(128)}, f32[32,1,256]{2,1,0:T(1,128)S(1)}, f32[16,32,1,16]{1,3,2,0:T(8,128)}, f32[16,32,1,16]{1,3,2,0:T(8,128)S(1)}, s32[]{:T(128)}, ...), condition=%wide.region_2.3_spmd.clone, body=%wide.region_1.2_spmd.clone.sunk | while | flops 1731587 | bytes 217183 | solution.py:39
  387.0 15.7 %all-gather.3 = f32[512,1,16]{2,1,0:T(1,128)S(1)} all-gather(f32[32,1,16]{2,1,0:T(1,128)S(1)} %get-tuple-element.824), channel_id=5, replica_groups=mesh['replica'=16,'fsdp'=4,'tensor'=4] {'replica'}, dimensions={0}, use_global_device_ids=true | all-gather | bytes 34816 | tf_op jit(solution)/shard_map/all_gather | solution.py:86
  402.9 10.4 %while.105 = (s32[]{:T(128)}, f32[32,1,256]{2,1,0:T(1,128)S(1)}, f32[16,32,1,16]{1,3,2,0:T(8,128)S(1)}, f32[16,32,1,16]{1,3,2,0:T(8,128)S(1)}, s32[]{:T(128)}, /*index=5*/s32[]{:T(128)}) while((s32[]{:T(128)}, f32[32,1,256]{2,1,0:T(1,128)S(1)}, f32[16,32,1,16]{1,3,2,0:T(8,128)S(1)}, f32[16,32,1,16]{1,3,2,0:T(8,128)S(1)}, ...), condition=%wide.region_4.5_spmd.clone, body=%wide.region_3.4_spmd.clone.sunk | while | flops 1731587 | bytes 217183 | solution.py:39
  414.0 16.0 %all-gather.5 = f32[512,1,16]{2,1,0:T(1,128)S(1)} all-gather(f32[32,1,16]{2,1,0:T(1,128)S(1)} %get-tuple-element.823), channel_id=7, replica_groups=mesh['replica'=16,'fsdp'=4,'tensor'=4] {'replica'}, dimensions={0}, use_global_device_ids=true | all-gather | bytes 34816 | tf_op jit(solution)/shard_map/all_gather | solution.py:86
  430.1 10.4 %while.106 = (s32[]{:T(128)}, f32[32,1,256]{2,1,0:T(1,128)S(1)}, f32[16,32,1,16]{1,3,2,0:T(8,128)S(1)}, f32[16,32,1,16]{1,3,2,0:T(8,128)S(1)}, s32[]{:T(128)}, /*index=5*/s32[]{:T(128)}) while((s32[]{:T(128)}, f32[32,1,256]{2,1,0:T(1,128)S(1)}, f32[16,32,1,16]{1,3,2,0:T(8,128)S(1)}, f32[16,32,1,16]{1,3,2,0:T(8,128)S(1)}, ...), condition=%wide.region_6.7_spmd.clone, body=%wide.region_5.6_spmd.clone.sunk | while | flops 1731587 | bytes 217183 | solution.py:39
  441.2 15.7 %all-gather.7 = f32[512,1,16]{2,1,0:T(1,128)S(1)} all-gather(f32[32,1,16]{2,1,0:T(1,128)S(1)} %get-tuple-element.822), channel_id=9, replica_groups=mesh['replica'=16,'fsdp'=4,'tensor'=4] {'replica'}, dimensions={0}, use_global_device_ids=true | all-gather | bytes 34816 | tf_op jit(solution)/shard_map/all_gather | solution.py:86
  457.1 10.4 %while.107 = (s32[]{:T(128)}, f32[32,1,256]{2,1,0:T(1,128)S(1)}, f32[16,32,1,16]{1,3,2,0:T(8,128)S(1)}, f32[16,32,1,16]{1,3,2,0:T(8,128)S(1)}, s32[]{:T(128)}, /*index=5*/s32[]{:T(128)}) while((s32[]{:T(128)}, f32[32,1,256]{2,1,0:T(1,128)S(1)}, f32[16,32,1,16]{1,3,2,0:T(8,128)S(1)}, f32[16,32,1,16]{1,3,2,0:T(8,128)S(1)}, ...), condition=%wide.region_8.9_spmd.clone, body=%wide.region_7.8_spmd.clone.sunk | while | flops 1731587 | bytes 217183 | solution.py:39
  468.2 16.0 %all-gather.9 = f32[512,1,16]{2,1,0:T(1,128)S(1)} all-gather(f32[32,1,16]{2,1,0:T(1,128)S(1)} %get-tuple-element.821), channel_id=11, replica_groups=mesh['replica'=16,'fsdp'=4,'tensor'=4] {'replica'}, dimensions={0}, use_global_device_ids=true | all-gather | bytes 34816 | tf_op jit(solution)/shard_map/all_gather | solution.py:86
  484.3 10.4 %while.108 = (s32[]{:T(128)}, f32[32,1,256]{2,1,0:T(1,128)S(1)}, f32[16,32,1,16]{1,3,2,0:T(8,128)S(1)}, f32[16,32,1,16]{1,3,2,0:T(8,128)S(1)}, s32[]{:T(128)}, /*index=5*/s32[]{:T(128)}) while((s32[]{:T(128)}, f32[32,1,256]{2,1,0:T(1,128)S(1)}, f32[16,32,1,16]{1,3,2,0:T(8,128)S(1)}, f32[16,32,1,16]{1,3,2,0:T(8,128)S(1)}, ...), condition=%wide.region_10.11_spmd.clone, body=%wide.region_9.10_spmd.clone.sunk | while | flops 1731587 | bytes 217183 | solution.py:39
  495.4 15.7 %all-gather.11 = f32[512,1,16]{2,1,0:T(1,128)S(1)} all-gather(f32[32,1,16]{2,1,0:T(1,128)S(1)} %get-tuple-element.820), channel_id=13, replica_groups=mesh['replica'=16,'fsdp'=4,'tensor'=4] {'replica'}, dimensions={0}, use_global_device_ids=true | all-gather | bytes 34816 | tf_op jit(solution)/shard_map/all_gather | solution.py:86
  511.3 10.4 %while.109 = (s32[]{:T(128)}, f32[32,1,256]{2,1,0:T(1,128)S(1)}, f32[16,32,1,16]{1,3,2,0:T(8,128)S(1)}, f32[16,32,1,16]{1,3,2,0:T(8,128)S(1)}, s32[]{:T(128)}, /*index=5*/s32[]{:T(128)}) while((s32[]{:T(128)}, f32[32,1,256]{2,1,0:T(1,128)S(1)}, f32[16,32,1,16]{1,3,2,0:T(8,128)S(1)}, f32[16,32,1,16]{1,3,2,0:T(8,128)S(1)}, ...), condition=%wide.region_12.13_spmd.clone, body=%wide.region_11.12_spmd.clone.sunk | while | flops 1731587 | bytes 217183 | solution.py:39
  522.4 16.0 %all-gather.13 = f32[512,1,16]{2,1,0:T(1,128)S(1)} all-gather(f32[32,1,16]{2,1,0:T(1,128)S(1)} %get-tuple-element.819), channel_id=15, replica_groups=mesh['replica'=16,'fsdp'=4,'tensor'=4] {'replica'}, dimensions={0}, use_global_device_ids=true | all-gather | bytes 34816 | tf_op jit(solution)/shard_map/all_gather | solution.py:86
  538.5 10.4 %while.110 = (s32[]{:T(128)}, f32[32,1,256]{2,1,0:T(1,128)S(1)}, f32[16,32,1,16]{1,3,2,0:T(8,128)S(1)}, f32[16,32,1,16]{1,3,2,0:T(8,128)S(1)}, s32[]{:T(128)}, /*index=5*/s32[]{:T(128)}) while((s32[]{:T(128)}, f32[32,1,256]{2,1,0:T(1,128)S(1)}, f32[16,32,1,16]{1,3,2,0:T(8,128)S(1)}, f32[16,32,1,16]{1,3,2,0:T(8,128)S(1)}, ...), condition=%wide.region_14.15_spmd.clone, body=%wide.region_13.14_spmd.clone.sunk | while | flops 1731587 | bytes 217183 | solution.py:39
  549.7 15.7 %all-gather.15 = f32[512,1,16]{2,1,0:T(1,128)S(1)} all-gather(f32[32,1,16]{2,1,0:T(1,128)S(1)} %get-tuple-element.818), channel_id=17, replica_groups=mesh['replica'=16,'fsdp'=4,'tensor'=4] {'replica'}, dimensions={0}, use_global_device_ids=true | all-gather | bytes 34816 | tf_op jit(solution)/shard_map/all_gather | solution.py:86
  565.5 10.6 %while.111 = (s32[]{:T(128)}, f32[32,1,256]{2,1,0:T(1,128)S(1)}, f32[16,32,1,16]{1,3,2,0:T(8,128)S(1)}, f32[16,32,1,16]{1,3,2,0:T(8,128)S(1)}, s32[]{:T(128)}, /*index=5*/s32[]{:T(128)}) while((s32[]{:T(128)}, f32[32,1,256]{2,1,0:T(1,128)S(1)}, f32[16,32,1,16]{1,3,2,0:T(8,128)S(1)}, f32[16,32,1,16]{1,3,2,0:T(8,128)S(1)}, ...), condition=%wide.region_16.17_spmd.clone, body=%wide.region_15.16_spmd.clone.sunk | while | flops 1731587 | bytes 217183 | solution.py:39
  595.6 12.4 %copy.112 = bf16[32,64,8,64]{3,2,1,0:T(8,128)(2,1)} copy(bf16[32,64,8,64]{3,1,0,2:T(8,128)(2,1)} %fusion.119) | data formatting | bytes 4194304 | tf_op jit(solution)/shard_map/concatenate | solution.py:90
  (980 shorter events, 167.3 us)
Async XLA Ops:
  7.2 92.2 %copy-start = (bf16[512,512]{1,0:T(8,128)(2,1)S(1)}, bf16[512,512]{1,0:T(8,128)(2,1)}, u32[]{:S(2)}) copy-start(bf16[512,512]{1,0:T(8,128)(2,1)} %param.21) | copy-start | bytes 1572868
  7.2 92.1 %all-gather.18.cloned.1.call-start = ((), (), s32[]{:S(2)}) async-start(), calls=%async_computation.1 | async-start | bytes 10485760 | tf_op jit(solution)/shard_map/all_gather | solution.py:53
  7.9 254.8 %reduce-scatter.2.cloned.1.call-start = ((), (), s32[]{:S(2)}) async-start(), calls=%async_computation.2 | async-start | bytes 20971520 | tf_op jit(solution)/shard_map/reduce_scatter | solution.py:54
  111.0 0.8 copy-start.2
  595.6 18.8 %copy-start.1 = (bf16[512,512]{1,0:T(8,128)(2,1)S(1)}, bf16[512,512]{1,0:T(8,128)(2,1)}, u32[]{:S(2)}) copy-start(bf16[512,512]{1,0:T(8,128)(2,1)} %param.21) | copy-start | bytes 1572868
Sparse Core Ops, SparseCore 0:
  9.8 89.4 all-gather.17
  111.1 151.5 reduce-scatter.1
where the time goes:
time: 628 us; the launch traced here: 622 us
  blocking collectives  259 us (41%)
  matrix products  120 us (19%)
  waiting for transfers between devices  112 us (18%)
  local copies, waits for them, and re-layouts  76.4 us (12%)
  other arithmetic  35.3 us (6%)
  between operations  14.6 us (2%)
    all_gather x8, blocking collectives, local(): lax.all_gather(sent_index[None, :, column], 'replica', axis=0, tiled=True)  129 us
    all_gather x8, blocking collectives, local(): lax.all_gather(values[None, :, column], 'replica', axis=0, tiled=True)  129 us
    all_gather x1, waiting for transfers between devices, local(): gathered = lax.all_gather(activations, 'tensor', axis=0, tiled=True)  91.4 us
    dot_general x128, matrix products, add_replica(): jnp.einsum('abjc,abj->abc', onehot, replica_values, precision=lax.Precisi...  47.2 us
    dot_general x16, matrix products, decode(): jnp.einsum('ki,abkl,lj->aibj', cosine_rows, combined.reshape(span_rows, c...  24.8 us
    reduce_scatter x1, waiting for transfers between devices, local(): lax.psum_scatter(lax.dot_general(gathered, cotangent, contract_rows, pref...  19.5 us
    dot_general x2, matrix products, local(): jnp.einsum('ki,aibj,lj->abkl', cosine_rows, blocks, cosine_rows, precisio...  16.9 us
    dot_general x2, matrix products, local(): jnp.einsum('ki,abkl,lj->aibj', cosine_rows, kept_coeffs.reshape(span_rows...  15.3 us
  transfers between devices with their start and end apart: 2, of which 2 were waited for; matrix products, arithmetic and copies ran while one was open for 0% of the time, Pallas kernels for 0%

commit v1 on v0

v1 whole, which is shorter than its diff:
```python
import functools

import jax
import jax.numpy as jnp
import ml_dtypes
import numpy as np
from jax import lax
from jax.experimental import pallas as pl
from jax.experimental.pallas import tpu as pltpu
from jax.sharding import PartitionSpec as P

SPAN = 64
LOW = 16
TILE = 256
DECAY = 0.999
VMEM_LIMIT = 40 * 1024 * 1024


def split_table(table):
    high = table.astype(ml_dtypes.bfloat16)
    low = (table - high.astype(np.float64)).astype(ml_dtypes.bfloat16)
    return high, low


def tables(cols):
    frequency = np.arange(LOW)[:, None]
    position = np.arange(SPAN)[None, :]
    cosine = np.cos(np.pi * (2.0 * position + 1.0) * frequency / (2.0 * SPAN))
    cosine = cosine * np.where(frequency == 0, np.sqrt(1.0 / SPAN), np.sqrt(2.0 / SPAN))
    down_high, down_low = split_table(np.kron(np.eye(TILE // SPAN), cosine))
    across_high, across_low = split_table(np.kron(np.eye(cols // SPAN), cosine))
    return {
        "rows": np.concatenate([down_high, down_low], 0),
        "cols_high": np.ascontiguousarray(across_high.T),
        "cols_low": np.ascontiguousarray(across_low.T),
        "back_high": across_high,
        "back_low": across_low,
        "back_rows": np.concatenate([down_high.T, down_high.T, down_low.T], 1),
    }


def halves(x):
    high = x.astype(jnp.bfloat16)
    return high, (x - high.astype(jnp.float32)).astype(jnp.bfloat16)


def dot(a, b):
    return jnp.dot(a, b, preferred_element_type=jnp.float32)


def times_table(x, high, low):
    rows = x.shape[0]
    x_high, x_low = halves(x)
    both = dot(jnp.concatenate([x_high, x_low], 0), high)
    return both[:rows] + both[rows:] + dot(x_high, low)


def forward(x, rows_ref, cols_high_ref, cols_low_ref):
    x_high, x_low = halves(x)
    count = rows_ref.shape[0] // 2
    both = dot(rows_ref[...], x_high)
    down = both[:count] + both[count:] + dot(rows_ref[:count, :], x_low)
    return times_table(down, cols_high_ref[...], cols_low_ref[...])


def backward(coefficients, back_high_ref, back_low_ref, back_rows_ref):
    across = times_table(coefficients, back_high_ref[...], back_low_ref[...])
    high, low = halves(across)
    return dot(back_rows_ref[...], jnp.concatenate([high, low, high], 0))


def order_kernel(tensor_ref, *refs):
    parts, out_ref = refs[:4], refs[4]
    for shift in range(4):
        start = lax.rem(tensor_ref[0] + 4 - shift, 4) * 128
        for d in range(4):
            out_ref[pl.ds((shift * 4 + d) * 128, 128), :] = parts[d][pl.ds(pl.multiple_of(start, 128), 128), :]


def chunk_kernel(splits, first, *refs):
    own = refs[:4]
    others = refs[4 : 4 + 4 * splits]
    refs = refs[4 + 4 * splits :]
    cot_ref, momentum_ref, mask_ref, rows_ref, ch_ref, cl_ref, bh_ref, bl_ref, br_ref = refs[:9]
    new_ref, kept_ref, lhs = refs[-3:]
    step = pl.program_id(0)
    for shift in range(4):
        lhs[pl.ds(shift * 512, 128), :] = own[shift][...]
        if splits == 1:
            lhs[pl.ds(shift * 512 + 128, 384), :] = others[shift][...]
        else:
            for part in range(splits):

                @pl.when(step == part)
                def _():
                    lhs[pl.ds(shift * 512 + 128, 384), :] = others[part * 4 + shift][...]

    gradient = lax.dot_general(
        lhs[...], cot_ref[...], (((0,), (0,)), ((), ())), preferred_element_type=jnp.float32
    )
    blended = DECAY * momentum_ref[...] + gradient
    kept = forward(blended, rows_ref, ch_ref, cl_ref) * mask_ref[...]
    kept_ref[...] = kept
    new_ref[...] = blended - backward(kept, bh_ref, bl_ref, br_ref)


def whole(shape):
    return pl.BlockSpec(shape, lambda i: (0,) * len(shape))


def chunk(c, own, others, cot, momentum, mask, consts, previous):
    rows, cols = momentum.shape
    splits = len(others)
    steps = 2
    low_rows = TILE // SPAN * LOW
    low_cols = cols // SPAN * LOW
    in_specs = [pl.BlockSpec((128, TILE), lambda i: (0, 2 * c + i))] * 4
    if splits == 1:
        in_specs += [pl.BlockSpec((384, TILE), lambda i: (0, i))] * 4
    else:
        in_specs += [whole((384, TILE))] * (4 * splits)
    in_specs += [
        whole(cot.shape),
        pl.BlockSpec((TILE, cols), lambda i: (2 * c + i, 0)),
        pl.BlockSpec((low_rows, low_cols), lambda i: (2 * c + i, 0)),
    ]
    in_specs += [whole(x.shape) for x in consts]
    args = [*own, *[x for part in others for x in part], cot, momentum, mask, *consts]
    aliases = {}
    if previous is not None:
        in_specs.append(pl.BlockSpec(memory_space=pl.ANY))
        args.append(previous)
        aliases = {len(args) - 1: 0}
    return pl.pallas_call(
        functools.partial(chunk_kernel, splits, previous is None),
        grid=(steps,),
        in_specs=in_specs,
        out_specs=[
            pl.BlockSpec((TILE, cols), lambda i: (2 * c + i, 0)),
            pl.BlockSpec((low_rows, low_cols), lambda i: (i, 0)),
        ],
        out_shape=[
            jax.ShapeDtypeStruct((rows, cols), jnp.float32),
            jax.ShapeDtypeStruct((steps * low_rows, low_cols), jnp.float32),
        ],
        scratch_shapes=[pltpu.VMEM((2048, TILE), jnp.bfloat16)],
        input_output_aliases=aliases,
        compiler_params=pltpu.CompilerParams(vmem_limit_bytes=VMEM_LIMIT),
        cost_estimate=pl.CostEstimate(
            flops=2 * 2048 * 512 * cols * 2, bytes_accessed=6 * 2**20, transcendentals=0
        ),
        name=f"chunk{c}",
    )(*args)


def update_kernel(coefficients_ref, bh_ref, bl_ref, br_ref, *refs):
    out_ref = refs[-1]
    out_ref[...] = backward(coefficients_ref[...], bh_ref, bl_ref, br_ref).astype(out_ref.dtype)


def spread(start, coefficients, shape, consts, previous):
    rows, cols = shape
    low_rows = TILE // SPAN * LOW
    steps = coefficients.shape[0] // low_rows
    in_specs = [pl.BlockSpec((low_rows, coefficients.shape[1]), lambda i: (i, 0))]
    in_specs += [whole(x.shape) for x in consts]
    args = [coefficients, *consts]
    aliases = {}
    if previous is not None:
        in_specs.append(pl.BlockSpec(memory_space=pl.ANY))
        args.append(previous)
        aliases = {len(args) - 1: 0}
    return pl.pallas_call(
        update_kernel,
        grid=(steps,),
        in_specs=in_specs,
        out_specs=pl.BlockSpec((TILE, cols), lambda i: (start + i, 0)),
        out_shape=jax.ShapeDtypeStruct((rows, cols), jnp.bfloat16),
        input_output_aliases=aliases,
        compiler_params=pltpu.CompilerParams(vmem_limit_bytes=VMEM_LIMIT),
        cost_estimate=pl.CostEstimate(flops=steps * 10**8, bytes_accessed=steps * 2**18, transcendentals=0),
        name=f"spread{start}",
    )(*args)


def shifted(x, axis, by, count):
    return lax.ppermute(x, axis, [(i, (i + by) % count) for i in range(count)])


def around(x, right):
    plus = shifted(x, "tensor", 1, 4)
    minus = shifted(x, "tensor", -1, 4)
    far = shifted(plus, "tensor", 1, 4) if right else shifted(minus, "tensor", -1, 4)
    return [x, plus, far, minus]


def over_replicas(x):
    for bit in (1, 2, 4, 8):
        x = x + lax.ppermute(x, "replica", [(i, i ^ bit) for i in range(16)])
    return x


def band_mask(band_index, cols):
    span_rows, span_cols, band = band_index.shape
    wide = jnp.repeat(band_index.transpose(2, 0, 1), LOW, axis=2)
    k1 = jnp.arange(LOW, dtype=jnp.int32)[None, :, None]
    k2 = jnp.arange(span_cols * LOW, dtype=jnp.int32)[None, None, :] % LOW
    here = k1 * SPAN + k2
    hit = functools.reduce(jnp.logical_or, [wide[j][:, None, :] == here for j in range(band)])
    return hit.astype(jnp.float32).reshape(span_rows * LOW, span_cols * LOW)


def local(activations, cotangent, momentum, band_index):
    momentum = momentum[0]
    rows, cols = momentum.shape
    fsdp = lax.axis_index("fsdp")
    tensor = lax.axis_index("tensor")
    table = tables(cols)
    forward_consts = [jnp.asarray(table[k]) for k in ("rows", "cols_high", "cols_low")]
    backward_consts = [jnp.asarray(table[k]) for k in ("back_high", "back_low", "back_rows")]
    consts = forward_consts + backward_consts

    def columns(d, start, width):
        owner = lax.rem(fsdp + d, 4)
        return lax.dynamic_slice(activations, (0, owner * rows + start), (128, width))

    own = around(columns(0, 0, rows), True)
    early = [shifted(columns(d, 0, 512), "fsdp", d, 4) for d in (1, 2, 3)]
    late = [shifted(columns(d, 512, 1536), "fsdp", d, 4) for d in (1, 2, 3)]
    cot_plus = shifted(cotangent, "fsdp", 1, 4)
    cot_minus = shifted(cotangent, "fsdp", -1, 4)
    cot_far = shifted(cot_plus, "fsdp", 1, 4)

    def stacked(parts, start, width):
        return jnp.concatenate([p[:, start : start + width] for p in parts], 0)

    others = [
        [around(stacked(early, 0, 512), False)],
        [around(stacked(late, 0, 512), True)],
        [around(stacked(late, 512, 512), False)],
        [around(stacked(late, 1024, 256), True), around(stacked(late, 1280, 256), False)],
    ]

    cot = pl.pallas_call(
        order_kernel,
        in_specs=[pl.BlockSpec(memory_space=pltpu.SMEM)] + [pl.BlockSpec(memory_space=pltpu.VMEM)] * 4,
        out_specs=pl.BlockSpec(memory_space=pltpu.VMEM),
        out_shape=jax.ShapeDtypeStruct((2048, cols), jnp.bfloat16),
        compiler_params=pltpu.CompilerParams(vmem_limit_bytes=VMEM_LIMIT),
        name="order",
    )(tensor.reshape(1).astype(jnp.int32), cotangent, cot_plus, cot_far, cot_minus)

    mask = band_mask(band_index[0], cols)
    new_momentum, kept = None, []
    for c in range(4):
        new_momentum, kept_c = chunk(c, own, others[c], cot, momentum, mask, consts, new_momentum)
        kept.append(kept_c)
    first = over_replicas(jnp.concatenate(kept[:3], 0))
    last = over_replicas(kept[3])
    update = spread(0, first, (rows, cols), backward_consts, None)
    update = spread(6, last, (rows, cols), backward_consts, update)
    return (new_momentum[None], update)


def solution(mesh):
    in_specs = (
        P(("replica", "fsdp", "tensor"), None),
        P(("replica", "fsdp"), "tensor"),
        P("replica", "fsdp", "tensor"),
        P("replica", "fsdp", "tensor", None),
    )
    out_specs = (P("replica", "fsdp", "tensor"), P("fsdp", "tensor"))
    return jax.shard_map(local, mesh=mesh, in_specs=in_specs, out_specs=out_specs, check_vma=False)
```

time: 628 us -> 158 us (0.25)
  blocking collectives: 259 us -> 0 us
  matrix products: 120 us -> 0 us
  local copies, waits for them, and re-layouts: 76.4 us -> 14.4 us
  starting transfers between devices: 0.08 us -> 54.9 us
  waiting for transfers between devices: 112 us -> 62.2 us
  other arithmetic: 35.3 us -> 3.4 us
  Pallas kernels: 0 us -> 21.7 us
  between operations: 14.6 us -> 1.05 us
    all_gather x16 -> x0, blocking collectives: 259 us -> none  [the longest x8 129 us: local(): lax.all_gather(sent_index[None, :, column], 'replica', axis=0, tiled=True)]
    dot_general x151 -> x0, matrix products: 120 us -> none  [the longest x128 47.2 us: add_replica(): jnp.einsum('abjc,abj->abc', onehot, replica_values, precision=lax.Precisi...]
    all_gather x1 -> x0, waiting for transfers between devices: 91.4 us -> none  [local(): gathered = lax.all_gather(activations, 'tensor', axis=0, tiled=True)]
    ppermute x0 -> x35, waiting for transfers between devices: none -> 62.2 us  [the longest x27 42.4 us: shifted(): return lax.ppermute(x, axis, [(i, (i + by) % count) for i in range(count)])]
    ppermute x0 -> x35, starting transfers between devices: none -> 54.9 us  [the longest x27 29.2 us: shifted(): return lax.ppermute(x, axis, [(i, (i + by) % count) for i in range(count)])]
    add x258 -> x9, other arithmetic: 28.8 us -> 0.88 us  [the longest x1 0.76 us: band_mask(): here = k1 * SPAN + k2]
    pallas_call x0 -> x7, Pallas kernels: none -> 21.7 us  [the longest x4 16.3 us: chunk(): pl.pallas_call(functools.partial(chunk_kernel, splits, previous is None),...]
    reduce_scatter x1 -> x0, waiting for transfers between devices: 19.5 us -> none  [local(): lax.psum_scatter(lax.dot_general(gathered, cotangent, contract_rows, pref...]
  transfers between devices with their start and end apart: 2 -> 35, of which waited for: 2 -> 17; matrix products, arithmetic and copies ran while one was open for 0% -> 11% of each run, Pallas kernels for 0% -> 10%
where the time goes in v1:
time: 158 us
  waiting for transfers between devices  62.2 us (39%)
  starting transfers between devices  54.9 us (35%)
  Pallas kernels  21.7 us (14%)
  local copies, waits for them, and re-layouts  14.4 us (9%)
  other arithmetic  3.4 us (2%)
    ppermute x27, waiting for transfers between devices, shifted(): return lax.ppermute(x, axis, [(i, (i + by) % count) for i in range(count)])  42.4 us
    ppermute x27, starting transfers between devices, shifted(): return lax.ppermute(x, axis, [(i, (i + by) % count) for i in range(count)])  29.2 us
    ppermute x8, starting transfers between devices, over_replicas(): x = x + lax.ppermute(x, 'replica', [(i, i ^ bit) for i in range(16)])  25.7 us
    ppermute x8, waiting for transfers between devices, over_replicas(): x = x + lax.ppermute(x, 'replica', [(i, i ^ bit) for i in range(16)])  19.7 us
    pallas_call x4, Pallas kernels, chunk(): pl.pallas_call(functools.partial(chunk_kernel, splits, previous is None),...  16.3 us
    broadcast_in_dim x32, local copies, waits for them, and re-layouts, band_mask(): wide = jnp.repeat(band_index.transpose(2, 0, 1), LOW, axis=2)  5.71 us
    pallas_call x2, Pallas kernels, spread(): pl.pallas_call(update_kernel, grid=(steps,), in_specs=in_specs, out_specs...  5.29 us
    dynamic_slice x3, local copies, waits for them, and re-layouts, columns(): lax.dynamic_slice(activations, (0, owner * rows + start), (128, width))  4.21 us
  transfers between devices with their start and end apart: 35, of which 17 were waited for; matrix products, arithmetic and copies ran while one was open for 11% of the time, Pallas kernels for 10%

profile of v1, /device:TPU:1, one launch (start us, length us, event | category | flops | bytes accessed | tf_op | source)
XLA Modules:
  0.0 157.7 jit_solution(2372710359197506668)
XLA Ops:
  1.8 2.1 %collective-permute-start = (bf16[128,2048]{1,0:T(8,128)(2,1)S(1)}, bf16[128,2048]{1,0:T(8,128)(2,1)S(1)}, u32[]{:S(2)}, u32[]{:S(2)}) collective-permute-start(bf16[128,2048]{1,0:T(8,128)(2,1)S(1)} %constant_dynamic-slice_fusion.6.refs_0_), channel_id=1, source_target_pairs={{0,1},{1,2},{2,3},{3,0},{4,5},{5,6},{6,7},{7,4},{8,9},{9,10},{10,1... | collective-permute-start | bytes 1572872 | tf_op jit(solution)/shard_map/ppermute | solution.py:187
  5.3 1.8 %constant_dynamic-slice_fusion = (bf16[128,512]{1,0:T(8,128)(2,1)}, bf16[128,512]{1,0:T(8,128)(2,1)}, bf16[128,512]{1,0:T(8,128)(2,1)}) fusion(bf16[128,8192]{1,0:T(8,128)(2,1)} %param.10, s32[]{:T(128)S(6)} %select_n.70, s32[]{:T(128)S(6)} %select_n.68, s32[]{:T(128)S(6)} %select_n.69), kind=kLoop, calls=%fused_computation.14 | loop fusion | bytes 786444 | tf_op jit(solution)/shard_map/dynamic_slice | solution.py:225
  8.4 2.6 %collective-permute-start.22 = (bf16[128,512]{1,0:T(8,128)(2,1)}, bf16[128,512]{1,0:T(8,128)(2,1)}, u32[]{:S(2)}, u32[]{:S(2)}) collective-permute-start(bf16[128,512]{1,0:T(8,128)(2,1)} %get-tuple-element.20), channel_id=1, source_target_pairs={{0,8},{4,12},{8,0},{12,4},{1,9},{5,13},{9,1},{13,5},{2,10},{6,14},... | collective-permute-start | bytes 393224 | tf_op jit(solution)/shard_map/ppermute | solution.py:187
  22.1 2.7 %collective-permute-start.23 = (bf16[128,512]{1,0:T(8,128)(2,1)}, bf16[128,512]{1,0:T(8,128)(2,1)S(1)}, u32[]{:S(2)}, u32[]{:S(2)}) collective-permute-start(bf16[128,512]{1,0:T(8,128)(2,1)} %get-tuple-element.18), channel_id=1, source_target_pairs={{0,12},{4,0},{8,4},{12,8},{1,13},{5,1},{9,5},{13,9},{2,14},{6,2},{... | collective-permute-start | bytes 393224 | tf_op jit(solution)/shard_map/ppermute | solution.py:187
  28.2 3.2 %collective-permute-start.5 = (bf16[128,1536]{1,0:T(8,128)(2,1)S(1)}, bf16[128,1536]{1,0:T(8,128)(2,1)S(1)}, u32[]{:S(2)}, u32[]{:S(2)}) collective-permute-start(bf16[128,1536]{1,0:T(8,128)(2,1)S(1)} %get-tuple-element.22), channel_id=1, source_target_pairs={{0,12},{4,0},{8,4},{12,8},{1,13},{5,1},{9,5},{13,9},{2,14},{6,2},{... | collective-permute-start | bytes 1179656 | tf_op jit(solution)/shard_map/ppermute | solution.py:187
  32.4 3.3 %collective-permute-done.4 = bf16[128,1536]{1,0:T(8,128)(2,1)S(1)} collective-permute-done((bf16[128,1536]{1,0:T(8,128)(2,1)S(1)}, bf16[128,1536]{1,0:T(8,128)(2,1)S(1)}, u32[]{:S(2)}, u32[]{:S(2)}) %collective-permute-start.4) | collective-permute-done | bytes 393248 | tf_op jit(solution)/shard_map/ppermute | solution.py:187
  37.0 6.7 %collective-permute-done.5 = bf16[128,1536]{1,0:T(8,128)(2,1)S(1)} collective-permute-done((bf16[128,1536]{1,0:T(8,128)(2,1)S(1)}, bf16[128,1536]{1,0:T(8,128)(2,1)S(1)}, u32[]{:S(2)}, u32[]{:S(2)}) %collective-permute-start.5) | collective-permute-done | bytes 393248 | tf_op jit(solution)/shard_map/ppermute | solution.py:187
  43.7 1.9 %collective-permute-start.14 = (bf16[512,512]{1,0:T(8,128)(2,1)S(1)}, bf16[512,512]{1,0:T(8,128)(2,1)S(1)}, u32[]{:S(2)}, u32[]{:S(2)}) collective-permute-start(bf16[512,512]{1,0:T(8,128)(2,1)S(1)} %copy-done.7), channel_id=1, source_target_pairs={{0,12},{4,0},{8,4},{12,8},{1,13},{5,1},{9,5},{13,9},{2,14},{6,2},{... | collective-permute-start | bytes 1572872 | tf_op jit(solution)/shard_map/ppermute | solution.py:187
  47.4 6.1 %collective-permute-done.24.refs_5_ = bf16[384,512]{1,0:T(8,128)(2,1)S(1)} collective-permute-done((bf16[384,512]{1,0:T(8,128)(2,1)S(1)}, bf16[384,512]{1,0:T(8,128)(2,1)S(1)}, u32[]{:S(2)}, u32[]{:S(2)}) %collective-permute-start.24) | collective-permute-done | bytes 393248 | tf_op jit(solution)/shard_map/ppermute | solution.py:187
  53.5 2.7 %collective-permute-start.16 = (bf16[384,512]{1,0:T(8,128)(2,1)S(1)}, bf16[384,512]{1,0:T(8,128)(2,1)S(1)}, u32[]{:S(2)}, u32[]{:S(2)}) collective-permute-start(bf16[384,512]{1,0:T(8,128)(2,1)S(1)} %pad_maximum_fusion.refs_4_), channel_id=1, source_target_pairs={{0,3},{1,0},{2,1},{3,2},{4,7},{5,4},{6,5},{7,6},{8,11},{9,8},{10,9... | collective-permute-start | bytes 1179656 | tf_op jit(solution)/shard_map/ppermute | solution.py:187
  57.7 7.0 %collective-permute-done.18.refs_5_ = bf16[384,512]{1,0:T(8,128)(2,1)S(1)} collective-permute-done((bf16[384,512]{1,0:T(8,128)(2,1)S(1)}, bf16[384,512]{1,0:T(8,128)(2,1)S(1)}, u32[]{:S(2)}, u32[]{:S(2)}) %collective-permute-start.18) | collective-permute-done | bytes 393248 | tf_op jit(solution)/shard_map/ppermute | solution.py:187
  66.6 2.6 %collective-permute-start.10 = (bf16[384,256]{1,0:T(8,128)(2,1)S(1)}, bf16[384,256]{1,0:T(8,128)(2,1)S(1)}, u32[]{:S(2)}, u32[]{:S(2)}) collective-permute-start(bf16[384,256]{1,0:T(8,128)(2,1)S(1)} %pad_maximum_fusion.3.refs_8_), channel_id=1, source_target_pairs={{0,3},{1,0},{2,1},{3,2},{4,7},{5,4},{6,5},{7,6},{8,11},{9,8},{10,9... | collective-permute-start | bytes 589832 | tf_op jit(solution)/shard_map/ppermute | solution.py:187
  69.2 3.1 %collective-permute-done.1.refs_2_ = bf16[128,2048]{1,0:T(8,128)(2,1)S(1)} collective-permute-done((bf16[128,2048]{1,0:T(8,128)(2,1)S(1)}, bf16[128,2048]{1,0:T(8,128)(2,1)S(1)}, u32[]{:S(2)}, u32[]{:S(2)}) %collective-permute-start.1) | collective-permute-done | bytes 524320 | tf_op jit(solution)/shard_map/ppermute | solution.py:187
  72.3 4.1 %chunk0.1 = (f32[2048,512]{1,0:T(8,128)}, f32[128,128]{1,0:T(8,128)S(1)}) custom-call(bf16[128,2048]{1,0:T(8,128)(2,1)S(1)} %constant_dynamic-slice_fusion.6.refs_0_, bf16[128,2048]{1,0:T(8,128)(2,1)S(1)} %collective-permute-done.refs_1_, bf16[128,2048]{1,0:T(8,128)(2,1)S(1)} %collective-permute-done.1.refs_2_, ...), custom_call_target="tpu_custom_call" | custom-call | flops 2147483648 | bytes 6291456 | tf_op jit(solution)/shard_map/chunk0/pallas_call | solution.py:134
  76.4 4.3 %collective-permute-done.19.refs_6_ = bf16[384,512]{1,0:T(8,128)(2,1)S(1)} collective-permute-done((bf16[384,512]{1,0:T(8,128)(2,1)S(1)}, bf16[384,512]{1,0:T(8,128)(2,1)S(1)}, u32[]{:S(2)}, u32[]{:S(2)}) %collective-permute-start.19) | collective-permute-done | bytes 393248 | tf_op jit(solution)/shard_map/ppermute | solution.py:187
  80.7 4.1 %chunk1.1 = (f32[2048,512]{1,0:T(8,128)}, f32[128,128]{1,0:T(8,128)S(1)}) custom-call(bf16[128,2048]{1,0:T(8,128)(2,1)S(1)} %constant_dynamic-slice_fusion.6.refs_0_, bf16[128,2048]{1,0:T(8,128)(2,1)S(1)} %collective-permute-done.refs_1_, bf16[128,2048]{1,0:T(8,128)(2,1)S(1)} %collective-permute-done.1.refs_2_, ...), custom_call_target="tpu_custom_call", output_to_operand_aliasing={{0}: (17, {})} | custom-call | flops 2147483648 | bytes 6291456 | tf_op jit(solution)/shard_map/chunk1/pallas_call | solution.py:134
  84.8 4.4 %collective-permute-done.15.refs_5_ = bf16[384,512]{1,0:T(8,128)(2,1)S(1)} collective-permute-done((bf16[384,512]{1,0:T(8,128)(2,1)S(1)}, bf16[384,512]{1,0:T(8,128)(2,1)S(1)}, u32[]{:S(2)}, u32[]{:S(2)}) %collective-permute-start.15) | collective-permute-done | bytes 393248 | tf_op jit(solution)/shard_map/ppermute | solution.py:187
  89.1 4.1 %chunk2.1 = (f32[2048,512]{1,0:T(8,128)}, f32[128,128]{1,0:T(8,128)S(1)}) custom-call(bf16[128,2048]{1,0:T(8,128)(2,1)S(1)} %constant_dynamic-slice_fusion.6.refs_0_, bf16[128,2048]{1,0:T(8,128)(2,1)S(1)} %collective-permute-done.refs_1_, bf16[128,2048]{1,0:T(8,128)(2,1)S(1)} %collective-permute-done.1.refs_2_, ...), custom_call_target="tpu_custom_call", output_to_operand_aliasing={{0}: (17, {})} | custom-call | flops 2147483648 | bytes 6291456 | tf_op jit(solution)/shard_map/chunk2/pallas_call | solution.py:134
  93.2 8.3 %collective-permute-start.31 = (f32[384,128]{1,0:T(8,128)S(1)}, f32[384,128]{1,0:T(8,128)S(1)}, u32[]{:S(2)}, u32[]{:S(2)}) collective-permute-start(f32[384,128]{1,0:T(8,128)S(1)} %constant_dynamic-update-slice_fusion.3), channel_id=1, source_target_pairs={{0,16},{16,0},{32,48},{48,32},{64,80},{80,64},{96,112},{112,96},{1... | collective-permute-start | bytes 589832 | tf_op jit(solution)/shard_map/ppermute | solution.py:199
  102.8 2.3 %collective-permute-start.32 = (f32[384,128]{1,0:T(8,128)S(1)}, f32[384,128]{1,0:T(8,128)S(1)}, u32[]{:S(2)}, u32[]{:S(2)}) collective-permute-start(f32[384,128]{1,0:T(8,128)S(1)} %add.242), channel_id=1, source_target_pairs={{0,32},{16,48},{32,0},{48,16},{64,96},{80,112},{96,64},{112,80},{1... | collective-permute-start | bytes 589832 | tf_op jit(solution)/shard_map/ppermute | solution.py:199
  106.1 1.7 %collective-permute-start.8 = (bf16[384,256]{1,0:T(8,128)(2,1)S(1)}, bf16[384,256]{1,0:T(8,128)(2,1)S(1)}, u32[]{:S(2)}, u32[]{:S(2)}) collective-permute-start(bf16[384,256]{1,0:T(8,128)(2,1)S(1)} %pad_maximum_fusion.2.refs_4_), channel_id=1, source_target_pairs={{0,3},{1,0},{2,1},{3,2},{4,7},{5,4},{6,5},{7,6},{8,11},{9,8},{10,9... | collective-permute-start | bytes 589832 | tf_op jit(solution)/shard_map/ppermute | solution.py:187
  107.8 1.5 collective-permute-done.6.refs_5_
  110.2 2.9 %collective-permute-start.33 = (f32[384,128]{1,0:T(8,128)S(1)}, f32[384,128]{1,0:T(8,128)S(1)}, u32[]{:S(2)}, u32[]{:S(2)}) collective-permute-start(f32[384,128]{1,0:T(8,128)S(1)} %add.243), channel_id=1, source_target_pairs={{0,64},{16,80},{32,96},{48,112},{64,0},{80,16},{96,32},{112,48},{1... | collective-permute-start | bytes 589832 | tf_op jit(solution)/shard_map/ppermute | solution.py:199
  113.6 2.2 %collective-permute-done.11.refs_10_ = bf16[384,256]{1,0:T(8,128)(2,1)S(1)} collective-permute-done((bf16[384,256]{1,0:T(8,128)(2,1)S(1)}, bf16[384,256]{1,0:T(8,128)(2,1)S(1)}, u32[]{:S(2)}, u32[]{:S(2)}) %collective-permute-start.11) | collective-permute-done | bytes 196640 | tf_op jit(solution)/shard_map/ppermute | solution.py:187
  117.2 4.1 %chunk3.1 = (f32[2048,512]{1,0:T(8,128)}, f32[128,128]{1,0:T(8,128)S(1)}) custom-call(bf16[128,2048]{1,0:T(8,128)(2,1)S(1)} %constant_dynamic-slice_fusion.6.refs_0_, bf16[128,2048]{1,0:T(8,128)(2,1)S(1)} %collective-permute-done.refs_1_, bf16[128,2048]{1,0:T(8,128)(2,1)S(1)} %collective-permute-done.1.refs_2_, ...), custom_call_target="tpu_custom_call", output_to_operand_aliasing={{0}: (21, {})} | custom-call | flops 2147483648 | bytes 6291456 | tf_op jit(solution)/shard_map/chunk3/pallas_call | solution.py:134
  123.6 1.8 %collective-permute-start.28 = (f32[128,128]{1,0:T(8,128)S(1)}, f32[128,128]{1,0:T(8,128)S(1)}, u32[]{:S(2)}, u32[]{:S(2)}) collective-permute-start(f32[128,128]{1,0:T(8,128)S(1)} %add.238), channel_id=1, source_target_pairs={{0,32},{16,48},{32,0},{48,16},{64,96},{80,112},{96,64},{112,80},{1... | collective-permute-start | bytes 196616 | tf_op jit(solution)/shard_map/ppermute | solution.py:199
  125.4 6.1 %collective-permute-start.34 = (f32[384,128]{1,0:T(8,128)S(1)}, f32[384,128]{1,0:T(8,128)S(1)}, u32[]{:S(2)}, u32[]{:S(2)}) collective-permute-start(f32[384,128]{1,0:T(8,128)S(1)} %add.244), channel_id=1, source_target_pairs={{0,128},{16,144},{32,160},{48,176},{64,192},{80,208},{96,224},{112... | collective-permute-start | bytes 589832 | tf_op jit(solution)/shard_map/ppermute | solution.py:199
  132.8 12.4 %collective-permute-done.29 = f32[128,128]{1,0:T(8,128)S(1)} collective-permute-done((f32[128,128]{1,0:T(8,128)S(1)}, f32[128,128]{1,0:T(8,128)S(1)}, u32[]{:S(2)}, u32[]{:S(2)}) %collective-permute-start.29) | collective-permute-done | bytes 65568 | tf_op jit(solution)/shard_map/ppermute | solution.py:199
  145.2 1.5 collective-permute-start.30
  146.7 5.6 %collective-permute-done.30 = f32[128,128]{1,0:T(8,128)S(1)} collective-permute-done((f32[128,128]{1,0:T(8,128)S(1)}, f32[128,128]{1,0:T(8,128)S(1)}, u32[]{:S(2)}, u32[]{:S(2)}) %collective-permute-start.30) | collective-permute-done | bytes 65568 | tf_op jit(solution)/shard_map/ppermute | solution.py:199
  152.4 3.8 %spread0.1.refs_0_ = bf16[2048,512]{1,0:T(8,128)(2,1)} custom-call(f32[384,128]{1,0:T(8,128)S(1)} %add.245.coefficients_ref, bf16[128,512]{1,0:T(8,128)(2,1)S(1)} %copy-done.1, bf16[128,512]{1,0:T(8,128)(2,1)S(1)} %copy-done.2, bf16[256,192]{1,0:T(8,128)(2,1)S(1)} %copy-done.3), custom_call_target="tpu_custom_call" | custom-call | flops 600000000 | bytes 1572864 | tf_op jit(solution)/shard_map/spread0/pallas_call | solution.py:173
  156.2 1.5 spread6.1
  (128 shorter events, 34.1 us)
Async XLA Ops:
  1.8 51.8 %collective-permute-start = (bf16[128,2048]{1,0:T(8,128)(2,1)S(1)}, bf16[128,2048]{1,0:T(8,128)(2,1)S(1)}, u32[]{:S(2)}, u32[]{:S(2)}) collective-permute-start(bf16[128,2048]{1,0:T(8,128)(2,1)S(1)} %constant_dynamic-slice_fusion.6.refs_0_), channel_id=1, source_target_pairs={{0,1},{1,2},{2,3},{3,0},{4,5},{5,6},{6,7},{7,4},{8,9},{9,10},{10,1... | collective-permute-start | bytes 1572872 | tf_op jit(solution)/shard_map/ppermute | solution.py:187
  3.9 52.3 %collective-permute-start.2 = (bf16[128,2048]{1,0:T(8,128)(2,1)S(1)}, bf16[128,2048]{1,0:T(8,128)(2,1)S(1)}, u32[]{:S(2)}, u32[]{:S(2)}) collective-permute-start(bf16[128,2048]{1,0:T(8,128)(2,1)S(1)} %constant_dynamic-slice_fusion.6.refs_0_), channel_id=1, source_target_pairs={{0,3},{1,0},{2,1},{3,2},{4,7},{5,4},{6,5},{7,6},{8,11},{9,8},{10,9... | collective-permute-start | bytes 1572872 | tf_op jit(solution)/shard_map/ppermute | solution.py:187
  7.0 15.1 %collective-permute-start.21 = (bf16[128,512]{1,0:T(8,128)(2,1)}, bf16[128,512]{1,0:T(8,128)(2,1)}, u32[]{:S(2)}, u32[]{:S(2)}) collective-permute-start(bf16[128,512]{1,0:T(8,128)(2,1)} %get-tuple-element.19), channel_id=1, source_target_pairs={{0,4},{4,8},{8,12},{12,0},{1,5},{5,9},{9,13},{13,1},{2,6},{6,10},{... | collective-permute-start | bytes 393224 | tf_op jit(solution)/shard_map/ppermute | solution.py:187
  8.4 17.4 %collective-permute-start.22 = (bf16[128,512]{1,0:T(8,128)(2,1)}, bf16[128,512]{1,0:T(8,128)(2,1)}, u32[]{:S(2)}, u32[]{:S(2)}) collective-permute-start(bf16[128,512]{1,0:T(8,128)(2,1)} %get-tuple-element.20), channel_id=1, source_target_pairs={{0,8},{4,12},{8,0},{12,4},{1,9},{5,13},{9,1},{13,5},{2,10},{6,14},... | collective-permute-start | bytes 393224 | tf_op jit(solution)/shard_map/ppermute | solution.py:187
  12.4 15.8 %collective-permute-start.3 = (bf16[128,1536]{1,0:T(8,128)(2,1)S(1)}, bf16[128,1536]{1,0:T(8,128)(2,1)}, u32[]{:S(2)}, u32[]{:S(2)}) collective-permute-start(bf16[128,1536]{1,0:T(8,128)(2,1)S(1)} %get-tuple-element.21), channel_id=1, source_target_pairs={{0,4},{4,8},{8,12},{12,0},{1,5},{5,9},{9,13},{13,1},{2,6},{6,10},{... | collective-permute-start | bytes 1179656 | tf_op jit(solution)/shard_map/ppermute | solution.py:187
  25.8 9.9 %collective-permute-start.4 = (bf16[128,1536]{1,0:T(8,128)(2,1)S(1)}, bf16[128,1536]{1,0:T(8,128)(2,1)S(1)}, u32[]{:S(2)}, u32[]{:S(2)}) collective-permute-start(bf16[128,1536]{1,0:T(8,128)(2,1)S(1)} %get-tuple-element.23), channel_id=1, source_target_pairs={{0,8},{4,12},{8,0},{12,4},{1,9},{5,13},{9,1},{13,5},{2,10},{6,14},... | collective-permute-start | bytes 1179656 | tf_op jit(solution)/shard_map/ppermute | solution.py:187
  28.2 19.2 %collective-permute-start.12 = (bf16[512,512]{1,0:T(8,128)(2,1)S(1)}, bf16[512,512]{1,0:T(8,128)(2,1)S(1)}, u32[]{:S(2)}, u32[]{:S(2)}) collective-permute-start(bf16[512,512]{1,0:T(8,128)(2,1)S(1)} %copy-done.7), channel_id=1, source_target_pairs={{0,4},{4,8},{8,12},{12,0},{1,5},{5,9},{9,13},{13,1},{2,6},{6,10},{... | collective-permute-start | bytes 1572872 | tf_op jit(solution)/shard_map/ppermute | solution.py:187
  28.2 15.4 %collective-permute-start.5 = (bf16[128,1536]{1,0:T(8,128)(2,1)S(1)}, bf16[128,1536]{1,0:T(8,128)(2,1)S(1)}, u32[]{:S(2)}, u32[]{:S(2)}) collective-permute-start(bf16[128,1536]{1,0:T(8,128)(2,1)S(1)} %get-tuple-element.22), channel_id=1, source_target_pairs={{0,12},{4,0},{8,4},{12,8},{1,13},{5,1},{9,5},{13,9},{2,14},{6,2},{... | collective-permute-start | bytes 1179656 | tf_op jit(solution)/shard_map/ppermute | solution.py:187
  35.7 9.9 %collective-permute-start.25 = (bf16[384,512]{1,0:T(8,128)(2,1)S(1)}, bf16[384,512]{1,0:T(8,128)(2,1)S(1)}, u32[]{:S(2)}, u32[]{:S(2)}) collective-permute-start(bf16[384,512]{1,0:T(8,128)(2,1)S(1)} %constant_dynamic-update-slice_fusion.refs_4_), channel_id=1, source_target_pairs={{0,3},{1,0},{2,1},{3,2},{4,7},{5,4},{6,5},{7,6},{8,11},{9,8},{10,9... | collective-permute-start | bytes 1179656 | tf_op jit(solution)/shard_map/ppermute | solution.py:187
  43.7 12.6 %collective-permute-start.14 = (bf16[512,512]{1,0:T(8,128)(2,1)S(1)}, bf16[512,512]{1,0:T(8,128)(2,1)S(1)}, u32[]{:S(2)}, u32[]{:S(2)}) collective-permute-start(bf16[512,512]{1,0:T(8,128)(2,1)S(1)} %copy-done.7), channel_id=1, source_target_pairs={{0,12},{4,0},{8,4},{12,8},{1,13},{5,1},{9,5},{13,9},{2,14},{6,2},{... | collective-permute-start | bytes 1572872 | tf_op jit(solution)/shard_map/ppermute | solution.py:187
  45.6 7.9 %collective-permute-start.24 = (bf16[384,512]{1,0:T(8,128)(2,1)S(1)}, bf16[384,512]{1,0:T(8,128)(2,1)S(1)}, u32[]{:S(2)}, u32[]{:S(2)}) collective-permute-start(bf16[384,512]{1,0:T(8,128)(2,1)S(1)} %constant_dynamic-update-slice_fusion.refs_4_), channel_id=1, source_target_pairs={{0,1},{1,2},{2,3},{3,0},{4,5},{5,6},{6,7},{7,4},{8,9},{9,10},{10,1... | collective-permute-start | bytes 1179656 | tf_op jit(solution)/shard_map/ppermute | solution.py:187
  47.4 17.4 %collective-permute-start.13 = (bf16[512,512]{1,0:T(8,128)(2,1)S(1)}, bf16[512,512]{1,0:T(8,128)(2,1)S(1)}, u32[]{:S(2)}, u32[]{:S(2)}) collective-permute-start(bf16[512,512]{1,0:T(8,128)(2,1)S(1)} %collective-permute-done.12.refs_1_), channel_id=1, source_target_pairs={{0,4},{4,8},{8,12},{12,0},{1,5},{5,9},{9,13},{13,1},{2,6},{6,10},{... | collective-permute-start | bytes 1572872 | tf_op jit(solution)/shard_map/ppermute | solution.py:187
  53.5 11.2 %collective-permute-start.18 = (bf16[384,512]{1,0:T(8,128)(2,1)S(1)}, bf16[384,512]{1,0:T(8,128)(2,1)S(1)}, u32[]{:S(2)}, u32[]{:S(2)}) collective-permute-start(bf16[384,512]{1,0:T(8,128)(2,1)S(1)} %pad_maximum_fusion.1.refs_4_), channel_id=1, source_target_pairs={{0,1},{1,2},{2,3},{3,0},{4,5},{5,6},{6,7},{7,4},{8,9},{9,10},{10,1... | collective-permute-start | bytes 1179656 | tf_op jit(solution)/shard_map/ppermute | solution.py:187
  53.5 12.9 %collective-permute-start.16 = (bf16[384,512]{1,0:T(8,128)(2,1)S(1)}, bf16[384,512]{1,0:T(8,128)(2,1)S(1)}, u32[]{:S(2)}, u32[]{:S(2)}) collective-permute-start(bf16[384,512]{1,0:T(8,128)(2,1)S(1)} %pad_maximum_fusion.refs_4_), channel_id=1, source_target_pairs={{0,3},{1,0},{2,1},{3,2},{4,7},{5,4},{6,5},{7,6},{8,11},{9,8},{10,9... | collective-permute-start | bytes 1179656 | tf_op jit(solution)/shard_map/ppermute | solution.py:187
  56.2 10.3 %collective-permute-start.26 = (bf16[384,512]{1,0:T(8,128)(2,1)S(1)}, bf16[384,512]{1,0:T(8,128)(2,1)S(1)}, u32[]{:S(2)}, u32[]{:S(2)}) collective-permute-start(bf16[384,512]{1,0:T(8,128)(2,1)S(1)} %collective-permute-done.25.refs_7_), channel_id=1, source_target_pairs={{0,3},{1,0},{2,1},{3,2},{4,7},{5,4},{6,5},{7,6},{8,11},{9,8},{10,9... | collective-permute-start | bytes 1179656 | tf_op jit(solution)/shard_map/ppermute | solution.py:187
  56.3 16.0 %collective-permute-start.1 = (bf16[128,2048]{1,0:T(8,128)(2,1)S(1)}, bf16[128,2048]{1,0:T(8,128)(2,1)S(1)}, u32[]{:S(2)}, u32[]{:S(2)}) collective-permute-start(bf16[128,2048]{1,0:T(8,128)(2,1)S(1)} %collective-permute-done.refs_1_), channel_id=1, source_target_pairs={{0,1},{1,2},{2,3},{3,0},{4,5},{5,6},{6,7},{7,4},{8,9},{9,10},{10,1... | collective-permute-start | bytes 1572872 | tf_op jit(solution)/shard_map/ppermute | solution.py:187
  64.8 11.7 %collective-permute-start.20 = (bf16[384,512]{1,0:T(8,128)(2,1)S(1)}, bf16[384,512]{1,0:T(8,128)(2,1)S(1)}, u32[]{:S(2)}, u32[]{:S(2)}) collective-permute-start(bf16[384,512]{1,0:T(8,128)(2,1)S(1)} %pad_maximum_fusion.1.refs_4_), channel_id=1, source_target_pairs={{0,3},{1,0},{2,1},{3,2},{4,7},{5,4},{6,5},{7,6},{8,11},{9,8},{10,9... | collective-permute-start | bytes 1179656 | tf_op jit(solution)/shard_map/ppermute | solution.py:187
  64.8 15.9 %collective-permute-start.19 = (bf16[384,512]{1,0:T(8,128)(2,1)S(1)}, bf16[384,512]{1,0:T(8,128)(2,1)S(1)}, u32[]{:S(2)}, u32[]{:S(2)}) collective-permute-start(bf16[384,512]{1,0:T(8,128)(2,1)S(1)} %collective-permute-done.18.refs_5_), channel_id=1, source_target_pairs={{0,1},{1,2},{2,3},{3,0},{4,5},{5,6},{6,7},{7,4},{8,9},{9,10},{10,1... | collective-permute-start | bytes 1179656 | tf_op jit(solution)/shard_map/ppermute | solution.py:187
  66.4 22.7 %collective-permute-start.15 = (bf16[384,512]{1,0:T(8,128)(2,1)S(1)}, bf16[384,512]{1,0:T(8,128)(2,1)S(1)}, u32[]{:S(2)}, u32[]{:S(2)}) collective-permute-start(bf16[384,512]{1,0:T(8,128)(2,1)S(1)} %pad_maximum_fusion.refs_4_), channel_id=1, source_target_pairs={{0,1},{1,2},{2,3},{3,0},{4,5},{5,6},{6,7},{7,4},{8,9},{9,10},{10,1... | collective-permute-start | bytes 1179656 | tf_op jit(solution)/shard_map/ppermute | solution.py:187
  66.6 41.3 %collective-permute-start.10 = (bf16[384,256]{1,0:T(8,128)(2,1)S(1)}, bf16[384,256]{1,0:T(8,128)(2,1)S(1)}, u32[]{:S(2)}, u32[]{:S(2)}) collective-permute-start(bf16[384,256]{1,0:T(8,128)(2,1)S(1)} %pad_maximum_fusion.3.refs_8_), channel_id=1, source_target_pairs={{0,3},{1,0},{2,1},{3,2},{4,7},{5,4},{6,5},{7,6},{8,11},{9,8},{10,9... | collective-permute-start | bytes 589832 | tf_op jit(solution)/shard_map/ppermute | solution.py:187
  72.3 16.9 %collective-permute-start.17 = (bf16[384,512]{1,0:T(8,128)(2,1)S(1)}, bf16[384,512]{1,0:T(8,128)(2,1)S(1)}, u32[]{:S(2)}, u32[]{:S(2)}) collective-permute-start(bf16[384,512]{1,0:T(8,128)(2,1)S(1)} %collective-permute-done.16.refs_7_), channel_id=1, source_target_pairs={{0,3},{1,0},{2,1},{3,2},{4,7},{5,4},{6,5},{7,6},{8,11},{9,8},{10,9... | collective-permute-start | bytes 1179656 | tf_op jit(solution)/shard_map/ppermute | solution.py:187
  93.2 9.6 %collective-permute-start.31 = (f32[384,128]{1,0:T(8,128)S(1)}, f32[384,128]{1,0:T(8,128)S(1)}, u32[]{:S(2)}, u32[]{:S(2)}) collective-permute-start(f32[384,128]{1,0:T(8,128)S(1)} %constant_dynamic-update-slice_fusion.3), channel_id=1, source_target_pairs={{0,16},{16,0},{32,48},{48,32},{64,80},{80,64},{96,112},{112,96},{1... | collective-permute-start | bytes 589832 | tf_op jit(solution)/shard_map/ppermute | solution.py:199
  101.5 7.8 %collective-permute-start.6 = (bf16[384,256]{1,0:T(8,128)(2,1)S(1)}, bf16[384,256]{1,0:T(8,128)(2,1)S(1)}, u32[]{:S(2)}, u32[]{:S(2)}) collective-permute-start(bf16[384,256]{1,0:T(8,128)(2,1)S(1)} %pad_maximum_fusion.2.refs_4_), channel_id=1, source_target_pairs={{0,1},{1,2},{2,3},{3,0},{4,5},{5,6},{6,7},{7,4},{8,9},{9,10},{10,1... | collective-permute-start | bytes 589832 | tf_op jit(solution)/shard_map/ppermute | solution.py:187
  102.8 7.4 %collective-permute-start.32 = (f32[384,128]{1,0:T(8,128)S(1)}, f32[384,128]{1,0:T(8,128)S(1)}, u32[]{:S(2)}, u32[]{:S(2)}) collective-permute-start(f32[384,128]{1,0:T(8,128)S(1)} %add.242), channel_id=1, source_target_pairs={{0,32},{16,48},{32,0},{48,16},{64,96},{80,112},{96,64},{112,80},{1... | collective-permute-start | bytes 589832 | tf_op jit(solution)/shard_map/ppermute | solution.py:199
  105.1 8.4 %collective-permute-start.9 = (bf16[384,256]{1,0:T(8,128)(2,1)S(1)}, bf16[384,256]{1,0:T(8,128)(2,1)S(1)}, u32[]{:S(2)}, u32[]{:S(2)}) collective-permute-start(bf16[384,256]{1,0:T(8,128)(2,1)S(1)} %pad_maximum_fusion.3.refs_8_), channel_id=1, source_target_pairs={{0,1},{1,2},{2,3},{3,0},{4,5},{5,6},{6,7},{7,4},{8,9},{9,10},{10,1... | collective-permute-start | bytes 589832 | tf_op jit(solution)/shard_map/ppermute | solution.py:187
  106.1 7.5 %collective-permute-start.8 = (bf16[384,256]{1,0:T(8,128)(2,1)S(1)}, bf16[384,256]{1,0:T(8,128)(2,1)S(1)}, u32[]{:S(2)}, u32[]{:S(2)}) collective-permute-start(bf16[384,256]{1,0:T(8,128)(2,1)S(1)} %pad_maximum_fusion.2.refs_4_), channel_id=1, source_target_pairs={{0,3},{1,0},{2,1},{3,2},{4,7},{5,4},{6,5},{7,6},{8,11},{9,8},{10,9... | collective-permute-start | bytes 589832 | tf_op jit(solution)/shard_map/ppermute | solution.py:187
  107.8 8.0 %collective-permute-start.11 = (bf16[384,256]{1,0:T(8,128)(2,1)S(1)}, bf16[384,256]{1,0:T(8,128)(2,1)S(1)}, u32[]{:S(2)}, u32[]{:S(2)}) collective-permute-start(bf16[384,256]{1,0:T(8,128)(2,1)S(1)} %collective-permute-done.10.refs_11_), channel_id=1, source_target_pairs={{0,3},{1,0},{2,1},{3,2},{4,7},{5,4},{6,5},{7,6},{8,11},{9,8},{10,9... | collective-permute-start | bytes 589832 | tf_op jit(solution)/shard_map/ppermute | solution.py:187
  109.4 7.8 %collective-permute-start.7 = (bf16[384,256]{1,0:T(8,128)(2,1)S(1)}, bf16[384,256]{1,0:T(8,128)(2,1)S(1)}, u32[]{:S(2)}, u32[]{:S(2)}) collective-permute-start(bf16[384,256]{1,0:T(8,128)(2,1)S(1)} %collective-permute-done.6.refs_5_), channel_id=1, source_target_pairs={{0,1},{1,2},{2,3},{3,0},{4,5},{5,6},{6,7},{7,4},{8,9},{9,10},{10,1... | collective-permute-start | bytes 589832 | tf_op jit(solution)/shard_map/ppermute | solution.py:187
  110.2 15.2 %collective-permute-start.33 = (f32[384,128]{1,0:T(8,128)S(1)}, f32[384,128]{1,0:T(8,128)S(1)}, u32[]{:S(2)}, u32[]{:S(2)}) collective-permute-start(f32[384,128]{1,0:T(8,128)S(1)} %add.243), channel_id=1, source_target_pairs={{0,64},{16,80},{32,96},{48,112},{64,0},{80,16},{96,32},{112,48},{1... | collective-permute-start | bytes 589832 | tf_op jit(solution)/shard_map/ppermute | solution.py:199
  123.6 8.0 %collective-permute-start.28 = (f32[128,128]{1,0:T(8,128)S(1)}, f32[128,128]{1,0:T(8,128)S(1)}, u32[]{:S(2)}, u32[]{:S(2)}) collective-permute-start(f32[128,128]{1,0:T(8,128)S(1)} %add.238), channel_id=1, source_target_pairs={{0,32},{16,48},{32,0},{48,16},{64,96},{80,112},{96,64},{112,80},{1... | collective-permute-start | bytes 196616 | tf_op jit(solution)/shard_map/ppermute | solution.py:199
  125.4 26.9 %collective-permute-start.34 = (f32[384,128]{1,0:T(8,128)S(1)}, f32[384,128]{1,0:T(8,128)S(1)}, u32[]{:S(2)}, u32[]{:S(2)}) collective-permute-start(f32[384,128]{1,0:T(8,128)S(1)} %add.244), channel_id=1, source_target_pairs={{0,128},{16,144},{32,160},{48,176},{64,192},{80,208},{96,224},{112... | collective-permute-start | bytes 589832 | tf_op jit(solution)/shard_map/ppermute | solution.py:199
  131.6 13.7 %collective-permute-start.29 = (f32[128,128]{1,0:T(8,128)S(1)}, f32[128,128]{1,0:T(8,128)S(1)}, u32[]{:S(2)}, u32[]{:S(2)}) collective-permute-start(f32[128,128]{1,0:T(8,128)S(1)} %add.239), channel_id=1, source_target_pairs={{0,64},{16,80},{32,96},{48,112},{64,0},{80,16},{96,32},{112,48},{1... | collective-permute-start | bytes 196616 | tf_op jit(solution)/shard_map/ppermute | solution.py:199
  (12 other events, 112.3 us)
